TPU v7x, 32 devices: a whole 2x2x4 slice. The times are simulated.
32 devices in a mesh: seq: 8 (over z, x), head: 4 (over y, core).
Axes of the slice: x: 2, y: 2, z: 4, core: 2. Of those that a mesh axis runs over, the one named last changes fastest.
Arguments:
- query_rows: bfloat16 [4096, 4096], P(('seq', 'head')), may hold values from -6 to 6
- key_rows: bfloat16 [4096, 4096], P(('seq', 'head')), may hold values from -6 to 6
- value_rows: bfloat16 [4096, 4096], P(('seq', 'head')), may hold values from -6 to 6
- residual: bfloat16 [4096, 5120], P('seq', 'head'), may hold values from -6 to 6
- out_weight: bfloat16 [4096, 5120], P(None, 'head'), may hold values from -0.09375 to 0.09375
- proj_first: bfloat16 [5120, 1024], P('head'), may hold values from -0.078125 to 0.078125
- proj_second: bfloat16 [1024, 1536], replicated, may hold values from -0.1875 to 0.1875
- dino_feats: bfloat16 [16, 64, 1536], P('seq', 'head'), may hold values from -60 to 60
- slot_frame: int32 [16], replicated, may hold values from 0 to 15, as said below
- patch_taps: int32 [4096, 4], P(('seq', 'head')), may hold values from 0 to 63
Outputs:
- hidden: bfloat16 [4096, 5120], P('seq', 'head')
- projected: bfloat16 [4096, 1536], P(('seq', 'head'))
- target: float32 [4096, 1536], P(('seq', 'head'))
- cosine: float32 [4096], P(('seq', 'head'))
Inputs may be any that keep to these rules, and one draw needn't show every extreme that they name: slot_frame is a permutation of the frames; the 2 slots of one seq index (slots i * 2 to (i + 1) * 2 - 1) hold frames of 2 different seq indices' tokens, where frames i * 2 to (i + 1) * 2 - 1 are those of seq index i's tokens.
All inputs are finite; a program needn't handle non-finite values.
Results may differ from a plain program's by a relative error of at most 0.0061.
Values may be sent and summed in bfloat16 or wider, within the bound.
A program may use at most 128 MiB of HBM per device.

v0:
```python
import jax
import jax.numpy as jnp
from jax import lax
from jax.sharding import PartitionSpec as P

HD = 128
PPF = 64
TAPS = 4
BLOCK = 512


def attend(operands):
    query_part, key_part, value_part = operands
    length = query_part.shape[0]
    item_count = query_part.shape[2]
    window_count = length // BLOCK
    score_scale = HD ** (-0.5)
    shaped = (
        query_part[:, 0].reshape(window_count, BLOCK, item_count, HD),
        key_part[:, 0].reshape(window_count, BLOCK, item_count, HD),
        value_part[:, 0].reshape(window_count, BLOCK, item_count, HD),
    )

    def one_window(parts):
        query_block, key_block, value_block = parts
        scores = (
            jnp.einsum("qhd,khd->hqk", query_block, key_block, preferred_element_type=jnp.float32)
            * score_scale
        )
        row_max = jnp.max(scores, axis=-1, keepdims=True)
        exponents = jnp.exp(scores - row_max)
        weights = (exponents / jnp.sum(exponents, axis=-1, keepdims=True)).astype(jnp.bfloat16)
        return jnp.einsum(
            "hqk,khd->qhd", weights, value_block, preferred_element_type=jnp.float32
        ).astype(jnp.bfloat16)

    return lax.map(one_window, shaped).reshape(length, 1, item_count, HD)


def per_device(
    query_rows,
    key_rows,
    value_rows,
    residual,
    out_weight,
    proj_first,
    proj_second,
    dino_feats,
    slot_frame,
    patch_taps,
):
    own_rows = query_rows.shape[0]
    group_count = lax.axis_size("head")
    per_group = query_rows.shape[1] // (HD * group_count)
    query_heads = query_rows.reshape(own_rows, group_count, per_group, HD)
    key_heads = key_rows.reshape(own_rows, group_count, per_group, HD)
    value_heads = value_rows.reshape(own_rows, group_count, per_group, HD)
    attended = attend(
        (
            lax.all_to_all(query_heads, "head", split_axis=1, concat_axis=0, tiled=True),
            lax.all_to_all(key_heads, "head", split_axis=1, concat_axis=0, tiled=True),
            lax.all_to_all(value_heads, "head", split_axis=1, concat_axis=0, tiled=True),
        )
    )
    seq_len = attended.shape[0]
    attended = attended.reshape(seq_len, per_group * HD)
    mixed_sum = jnp.dot(
        lax.all_gather(attended, "head", axis=1, tiled=True),
        out_weight,
        preferred_element_type=jnp.float32,
    )
    hidden = (residual.astype(jnp.float32) + mixed_sum).astype(jnp.bfloat16)
    pre_act = lax.psum_scatter(
        jnp.dot(hidden, proj_first, preferred_element_type=jnp.float32),
        "head",
        scatter_dimension=0,
        tiled=True,
    )
    lifted = jax.nn.silu(pre_act).astype(jnp.bfloat16)
    projected = jnp.dot(lifted, proj_second, preferred_element_type=jnp.float32).astype(
        jnp.bfloat16
    )
    seq_index = lax.axis_index("seq")
    head_index = lax.axis_index("head")
    frames_here = dino_feats.shape[0]
    wanted = seq_index * frames_here + jnp.arange(frames_here, dtype=jnp.int32)
    everything = lax.all_gather(dino_feats, "seq", axis=0, tiled=True)
    picker = (slot_frame[None, :] == wanted[:, None]).astype(jnp.bfloat16)
    frame_part = jnp.einsum(
        "ir,rpz->ipz", picker, everything, preferred_element_type=jnp.float32
    ).astype(jnp.bfloat16)
    whole_frames = lax.all_gather(frame_part, "head", axis=1, tiled=True)
    frame_feat = lax.dynamic_index_in_dim(whole_frames, head_index // 2, 0, keepdims=False)
    patch_ids = jnp.arange(PPF, dtype=jnp.int32)
    tap_counts = jnp.sum(
        (patch_taps[:, :, None] == patch_ids[None, None, :]).astype(jnp.float32), axis=1
    )
    target = jnp.dot(
        tap_counts.astype(jnp.bfloat16), frame_feat, preferred_element_type=jnp.float32
    ) * (1.0 / TAPS)
    proj_float = projected.astype(jnp.float32)
    inner = jnp.sum(proj_float * target, axis=-1)
    proj_sq = jnp.sum(proj_float * proj_float, axis=-1) + 1e-06
    target_sq = jnp.sum(target * target, axis=-1) + 1e-06
    cosine = inner / jnp.sqrt(proj_sq * target_sq)
    return (hidden, projected, target, cosine)


def solution(mesh):
    return jax.shard_map(
        per_device,
        mesh=mesh,
        in_specs=(
            P(("seq", "head"), None),
            P(("seq", "head"), None),
            P(("seq", "head"), None),
            P("seq", "head"),
            P(None, "head"),
            P("head", None),
            P(),
            P("seq", "head", None),
            P(),
            P(("seq", "head"), None),
        ),
        out_specs=(
            P("seq", "head"),
            P(("seq", "head"), None),
            P(("seq", "head"), None),
            P(("seq", "head")),
        ),
        check_vma=False,
    )
```

profile of v0, /device:TPU:0, one launch (start us, length us, event | category | flops | bytes accessed | tf_op | source)
XLA Modules:
  0.0 187.4 jit_solution(7240159391597058873)
XLA Ops:
  7.2 0.0 copy-start
  7.2 2.4 %copy.46 = bf16[128,4096]{0,1:T(8,128)(2,1)} copy(bf16[128,4096]{1,0:T(8,128)(2,1)} %param.10) | data formatting | bytes 2097152 | tf_op args[0]
  9.6 2.3 %copy.47 = bf16[128,4,8,128]{3,0,2,1:T(8,128)(2,1)} copy(bf16[128,4,8,128]{0,3,2,1:T(8,128)(2,1)} %bitcast.39) | data formatting | bytes 2097152 | tf_op jit(solution)/shard_map/reshape | solution.py:55
  11.9 4.2 %all-to-all-start = ((bf16[128,4,8,128]{3,0,2,1:T(8,128)(2,1)}), bf16[128,4,8,128]{3,0,2,1:T(8,128)(2,1)}, u32[]{:S(2)}, u32[]{:S(2)}) async-start(bf16[128,4,8,128]{3,0,2,1:T(8,128)(2,1)} %copy.47), calls=%async_computation | async-start | bytes 2097152 | tf_op jit(solution)/shard_map/all_to_all | solution.py:60
  16.1 2.3 %copy.49 = bf16[128,4096]{0,1:T(8,128)(2,1)} copy(bf16[128,4096]{1,0:T(8,128)(2,1)} %param.11) | data formatting | bytes 2097152 | tf_op args[1]
  18.4 2.3 %copy.50 = bf16[128,4,8,128]{3,0,2,1:T(8,128)(2,1)} copy(bf16[128,4,8,128]{0,3,2,1:T(8,128)(2,1)} %bitcast.40) | data formatting | bytes 2097152 | tf_op jit(solution)/shard_map/reshape | solution.py:56
  20.7 10.6 %all-to-all-done = bf16[128,4,8,128]{3,0,2,1:T(8,128)(2,1)} async-done(((bf16[128,4,8,128]{3,0,2,1:T(8,128)(2,1)}), bf16[128,4,8,128]{3,0,2,1:T(8,128)(2,1)}, u32[]{:S(2)}, u32[]{:S(2)}) %all-to-all-start) | async-done | bytes 1048608 | tf_op jit(solution)/shard_map/all_to_all | solution.py:60
  31.3 4.2 %all-to-all-start.1 = ((bf16[128,4,8,128]{3,0,2,1:T(8,128)(2,1)}), bf16[128,4,8,128]{3,0,2,1:T(8,128)(2,1)}, u32[]{:S(2)}, u32[]{:S(2)}) async-start(bf16[128,4,8,128]{3,0,2,1:T(8,128)(2,1)} %copy.50), calls=%async_computation.1 | async-start | bytes 2097152 | tf_op jit(solution)/shard_map/all_to_all | solution.py:61
  35.5 2.3 %copy.52 = bf16[128,4096]{0,1:T(8,128)(2,1)} copy(bf16[128,4096]{1,0:T(8,128)(2,1)} %param.12) | data formatting | bytes 2097152 | tf_op args[2]
  37.8 12.3 %all-to-all-done.1 = bf16[128,4,8,128]{3,0,2,1:T(8,128)(2,1)} async-done(((bf16[128,4,8,128]{3,0,2,1:T(8,128)(2,1)}), bf16[128,4,8,128]{3,0,2,1:T(8,128)(2,1)}, u32[]{:S(2)}, u32[]{:S(2)}) %all-to-all-start.1) | async-done | bytes 1048608 | tf_op jit(solution)/shard_map/all_to_all | solution.py:61
  50.1 4.3 %all-to-all-start.2 = ((bf16[128,4,8,128]{0,3,2,1:T(8,128)(2,1)}), bf16[128,4,8,128]{0,3,2,1:T(8,128)(2,1)}, u32[]{:S(2)}, u32[]{:S(2)}) async-start(bf16[128,4,8,128]{0,3,2,1:T(8,128)(2,1)} %bitcast.38), calls=%async_computation.2 | async-start | bytes 2097152 | tf_op jit(solution)/shard_map/all_to_all | solution.py:62
  54.4 0.0 all-gather.2.cloned.1.call-start
  54.4 2.4 %copy.48 = bf16[4,128,1,8,128]{4,1,0,3,2:T(8,128)(2,1)} copy(bf16[4,128,1,8,128]{4,1,3,0,2:T(8,128)(2,1)} %bitcast.2) | data formatting | bytes 2097152 | tf_op jit(solution)/shard_map/all_to_all | solution.py:60
  56.8 2.3 %copy.51 = bf16[4,128,1,8,128]{4,1,0,3,2:T(8,128)(2,1)} copy(bf16[4,128,1,8,128]{4,1,3,0,2:T(8,128)(2,1)} %bitcast.6) | data formatting | bytes 2097152 | tf_op jit(solution)/shard_map/all_to_all | solution.py:61
  59.1 9.8 %all-to-all-done.2 = bf16[128,4,8,128]{0,3,2,1:T(8,128)(2,1)} async-done(((bf16[128,4,8,128]{0,3,2,1:T(8,128)(2,1)}), bf16[128,4,8,128]{0,3,2,1:T(8,128)(2,1)}, u32[]{:S(2)}, u32[]{:S(2)}) %all-to-all-start.2) | async-done | bytes 1048608 | tf_op jit(solution)/shard_map/all_to_all | solution.py:62
  68.9 3.0 %copy.53 = bf16[4,128,1,8,128]{1,0,4,3,2:T(4,128)(2,1)} copy(bf16[4,128,1,8,128]{1,4,3,0,2:T(8,128)(2,1)} %bitcast.10) | data formatting | bytes 2097152 | tf_op jit(solution)/shard_map/all_to_all | solution.py:62
  71.9 2.3 %squeeze.19 = bf16[512,8,128]{0,2,1:T(8,128)(2,1)} reshape(bf16[4,128,1,8,128]{1,0,4,3,2:T(4,128)(2,1)} %copy.53) | data formatting | bytes 2097152 | tf_op jit(solution)/shard_map/while/body/jit(dynamic_index_in_dim)/squeeze | solution.py:37
  74.2 7.4 %fusion.21 = (f32[8,512]{1,0:T(8,128)S(1)}, f32[8,512,512]{1,2,0:T(8,128)}) fusion(bf16[512,8,128]{2,0,1:T(8,128)(2,1)} %bitcast.41, bf16[512,8,128]{2,0,1:T(8,128)(2,1)} %bitcast.42), kind=kOutput, calls=%fused_computation.35 | convolution fusion | flops 543162880 | bytes 10502144 | tf_op jit(solution)/shard_map/while/body/eval_jaxpr/sub | solution.py:31
  81.6 5.4 %fusion.7 = bf16[8,512,128]{1,2,0:T(8,128)(2,1)} fusion(bf16[512,8,128]{0,2,1:T(8,128)(2,1)} %squeeze.19, f32[8,512,512]{1,2,0:T(8,128)} %get-tuple-element.23, f32[8,512]{1,0:T(8,128)S(1)} %get-tuple-element.22), kind=kOutput, calls=%fused_computation.12 | convolution fusion | flops 541589504 | bytes 10502144 | tf_op jit(solution)/shard_map/while/body/eval_jaxpr/hqk,khd->qhd/dot_general | solution.py:33
  87.0 0.0 all-gather.2.cloned.1.call-update
  87.0 0.0 reduce-scatter.2.cloned.1.call-start
  87.1 35.7 %all-gather.2.cloned.1.call-done = bf16[512,4096]{0,1:T(8,128)(2,1)} async-done(((bf16[512,1024]{0,1:T(8,128)(2,1)}), bf16[512,4096]{0,1:T(8,128)(2,1)}) %all-gather.2.cloned.1.call-update) | async-done | bytes 4194320 | tf_op jit(solution)/shard_map/all_gather | solution.py:68
  122.8 0.0 copy-start.4
  122.8 10.8 %fusion.6 = bf16[512,1280]{1,0:T(8,128)(2,1)S(1)} fusion(bf16[512,4096]{0,1:T(8,128)(2,1)} %all-gather.2.cloned.1.call-done, bf16[4096,1280]{1,0:T(8,128)(2,1)} %param.14, bf16[512,1280]{1,0:T(8,128)(2,1)} %param.13), kind=kOutput, calls=%fused_computation.8 | convolution fusion | flops 5370675200 | bytes 17301504 | tf_op jit(solution)/shard_map/dot_general | solution.py:67
  133.6 0.0 copy-start.5
  133.6 1.0 copy-done.5
  134.7 0.0 copy-done.4
  134.7 0.0 copy-start.2
  134.7 0.0 copy-start.1
  134.7 0.0 copy-start.3
  134.7 2.9 %fusion.22 = f32[512,1024]{1,0:T(8,128)} fusion(bf16[512,1280]{1,0:T(8,128)(2,1)S(1)} %fusion.6, bf16[1280,1024]{1,0:T(8,128)(2,1)S(1)} %copy-done.4), kind=kOutput, calls=%fused_computation.36 | convolution fusion | flops 1342177280 | bytes 6029312 | tf_op jit(solution)/shard_map/dot_general | solution.py:74
  137.6 0.0 reduce-scatter.2.cloned.1.call-update
  137.6 0.0 copy-done.2
  137.7 0.0 copy-done.1
  137.7 32.3 %all_gather.10 = bf16[16,16,1536]{2,1,0:T(8,128)(2,1)S(1)} all-gather(bf16[2,16,1536]{2,1,0:T(8,128)(2,1)S(1)} %copy-done.1), channel_id=1, replica_groups=mesh['seq'=8,'head'=4] {'seq'}, dimensions={0}, use_global_device_ids=true | all-gather | bytes 884736 | tf_op jit(solution)/shard_map/all_gather | solution.py:87
  169.9 0.0 copy-done.3
  170.0 0.5 convolution_convert_fusion.1
  170.5 6.1 %all_gather.11 = bf16[2,64,1536]{2,0,1:T(2,128)(2,1)S(1)} all-gather(bf16[2,16,1536]{2,0,1:T(2,128)(2,1)S(1)} %convolution_convert_fusion.1), channel_id=1, replica_groups=mesh['seq'=8,'head'=4] {'head'}, dimensions={1}, use_global_device_ids=true | all-gather | bytes 491520 | tf_op jit(solution)/shard_map/all_gather | solution.py:92
  176.7 0.4 constant_dynamic-slice_fusion
  177.1 0.0 reduce-scatter.2.cloned.1.call-done
  177.1 0.0 copy-done
  177.1 1.6 convolution_convert_fusion
  178.8 0.0 copy-start.6
  178.8 1.2 multiply_reduce_fusion.1
  180.0 0.5 rsqrt_multiply_fusion
  180.5 0.0 copy-done.6
  (2 shorter events, 0.0 us)
Async XLA Ops:
  7.2 169.9 %copy-start = (bf16[1024,1536]{1,0:T(8,128)(2,1)S(1)}, bf16[1024,1536]{1,0:T(8,128)(2,1)}, u32[]{:S(2)}) copy-start(bf16[1024,1536]{1,0:T(8,128)(2,1)} %param.16) | copy-start | bytes 9437188
  11.9 19.4 %all-to-all-start = ((bf16[128,4,8,128]{3,0,2,1:T(8,128)(2,1)}), bf16[128,4,8,128]{3,0,2,1:T(8,128)(2,1)}, u32[]{:S(2)}, u32[]{:S(2)}) async-start(bf16[128,4,8,128]{3,0,2,1:T(8,128)(2,1)} %copy.47), calls=%async_computation | async-start | bytes 2097152 | tf_op jit(solution)/shard_map/all_to_all | solution.py:60
  31.3 18.8 %all-to-all-start.1 = ((bf16[128,4,8,128]{3,0,2,1:T(8,128)(2,1)}), bf16[128,4,8,128]{3,0,2,1:T(8,128)(2,1)}, u32[]{:S(2)}, u32[]{:S(2)}) async-start(bf16[128,4,8,128]{3,0,2,1:T(8,128)(2,1)} %copy.50), calls=%async_computation.1 | async-start | bytes 2097152 | tf_op jit(solution)/shard_map/all_to_all | solution.py:61
  50.1 18.8 %all-to-all-start.2 = ((bf16[128,4,8,128]{0,3,2,1:T(8,128)(2,1)}), bf16[128,4,8,128]{0,3,2,1:T(8,128)(2,1)}, u32[]{:S(2)}, u32[]{:S(2)}) async-start(bf16[128,4,8,128]{0,3,2,1:T(8,128)(2,1)} %bitcast.38), calls=%async_computation.2 | async-start | bytes 2097152 | tf_op jit(solution)/shard_map/all_to_all | solution.py:62
  54.4 68.4 %all-gather.2.cloned.1.call-start = ((), (), s32[]{:S(2)}) async-start(), calls=%async_computation.4 | async-start | bytes 5242880 | tf_op jit(solution)/shard_map/all_gather | solution.py:68
  87.0 90.0 %reduce-scatter.2.cloned.1.call-start = ((), (), s32[]{:S(2)}) async-start(), calls=%async_computation.5 | async-start | bytes 2621440 | tf_op jit(solution)/shard_map/reduce_scatter | solution.py:73
  122.8 11.9 %copy-start.4 = (bf16[1280,1024]{1,0:T(8,128)(2,1)S(1)}, bf16[1280,1024]{1,0:T(8,128)(2,1)}, u32[]{:S(2)}) copy-start(bf16[1280,1024]{1,0:T(8,128)(2,1)} %param.15) | copy-start | bytes 7864324
  133.6 1.1 copy-start.5
  134.7 2.9 %copy-start.2 = (s32[128,4]{0,1:T(4,128)S(1)}, s32[128,4]{0,1:T(4,128)}, u32[]{:S(2)}) copy-start(s32[128,4]{0,1:T(4,128)} %param.19) | copy-start | bytes 6148
  134.7 3.0 %copy-start.1 = (bf16[2,16,1536]{2,1,0:T(8,128)(2,1)S(1)}, bf16[2,16,1536]{2,1,0:T(8,128)(2,1)}, u32[]{:S(2)}) copy-start(bf16[2,16,1536]{2,1,0:T(8,128)(2,1)} %param.17) | copy-start | bytes 294916
  134.7 35.3 %copy-start.3 = (s32[16]{0:T(128)S(1)}, s32[16]{0:T(128)}, u32[]{:S(2)}) copy-start(s32[16]{0:T(128)} %param.18) | copy-start | bytes 196
  178.8 1.8 copy-start.6
Sparse Core Ops, SparseCore 0:
  87.2 35.5 all-gather.1
  137.7 31.4 reduce-scatter.1
where the time goes:
time: 188 us; the launch traced here: 187 us
  waiting for transfers between devices  68.4 us (36%)
  blocking collectives  38.4 us (20%)
  matrix products  30 us (16%)
  local copies, waits for them, and re-layouts  23 us (12%)
  between operations  14.2 us (8%)
  starting transfers between devices  12.9 us (7%)
    all_gather x1, waiting for transfers between devices, per_device(): lax.all_gather(attended, 'head', axis=1, tiled=True)  35.7 us
    all_gather x1, blocking collectives, per_device(): everything = lax.all_gather(dino_feats, 'seq', axis=0, tiled=True)  32.3 us
    all_to_all x1, waiting for transfers between devices, per_device(): lax.all_to_all(key_heads, 'head', split_axis=1, concat_axis=0, tiled=True)  12.3 us
    dot_general x1, matrix products, per_device(): jnp.dot(lax.all_gather(attended, 'head', axis=1, tiled=True), out_weight,...  10.8 us
    all_to_all x1, waiting for transfers between devices, per_device(): lax.all_to_all(query_heads, 'head', split_axis=1, concat_axis=0, tiled=True)  10.6 us
    all_to_all x1, waiting for transfers between devices, per_device(): lax.all_to_all(value_heads, 'head', split_axis=1, concat_axis=0, tiled=True)  9.76 us
    unnamed x17, local copies, waits for them, and re-layouts  8.03 us
    sub x1, matrix products, one_window(): exponents = jnp.exp(scores - row_max)  7.44 us
  transfers between devices with their start and end apart: 5, of which 4 were waited for; matrix products, arithmetic and copies ran while one was open for 7% of the time, Pallas kernels for 0%

commit v1 on v0

--- a/solution.py
+++ b/solution.py
@@ -1,6 +1,10 @@
+import functools
+
 import jax
 import jax.numpy as jnp
 from jax import lax
+from jax.experimental import pallas as pl
+from jax.experimental.pallas import tpu as pltpu
 from jax.sharding import PartitionSpec as P
 
 HD = 128
@@ -106,9 +110,482 @@
     return (hidden, projected, target, cosine)
 
 
+CHUNK_HEADS = 2
+MESH = pl.DeviceIdType.MESH
+
+
+def fused_kernel(
+    seq_count,
+    q_ref,
+    k_ref,
+    v_ref,
+    res_ref,
+    w_ref,
+    p1_ref,
+    p2_ref,
+    dino_ref,
+    slot_ref,
+    taps_ref,
+    hid_out,
+    proj_out,
+    targ_out,
+    cos_out,
+    qkv,
+    att,
+    acc,
+    w_v,
+    p1_v,
+    p2_v,
+    res_v,
+    hid_v,
+    pre_v,
+    lift_v,
+    part_send,
+    part_recv,
+    dino_all,
+    frame_sel,
+    frame_buf,
+    load_sem,
+    own_sem,
+    qkv_send,
+    qkv_recv,
+    att_send,
+    att_recv,
+    fwd_send,
+    fwd_recv,
+    part_ssem,
+    part_rsem,
+    dino_send,
+    dino_recv,
+    frame_send,
+    frame_recv,
+    hid_sem,
+):
+    seq = lax.axis_index("seq")
+    me = lax.axis_index("head")
+    chip = lax.div(me, 2)
+    core = lax.rem(me, 2)
+    sib = 2 * chip + (1 - core)
+    cross = 2 * (1 - chip) + core
+    diag = 2 * (1 - chip) + (1 - core)
+    peers = (sib, cross, diag)
+    rows = q_ref.shape[0]
+    tokens = 4 * rows
+    head_cols = q_ref.shape[1] // 4
+    chunks = qkv.shape[1]
+    width = qkv.shape[3]
+    wide = w_v.shape[1]
+    units = p1_v.shape[1]
+
+    barrier = pltpu.get_barrier_semaphore()
+    for peer in peers:
+        pl.semaphore_signal(barrier, inc=1, device_id={"head": peer}, device_id_type=MESH)
+    for step in range(1, seq_count):
+        other = lax.rem(seq + step, seq_count)
+        pl.semaphore_signal(barrier, inc=1, device_id={"seq": other}, device_id_type=MESH)
+    pl.semaphore_wait(barrier, 3 + seq_count - 1)
+
+    sources = (q_ref, k_ref, v_ref)
+    my_rows = pl.ds(pl.multiple_of(me * rows, rows), rows)
+
+    def columns(owner, i):
+        return pl.ds(pl.multiple_of(owner * head_cols + i * width, width), width)
+
+    qkv_copies = {}
+    own_copies = {}
+
+    def send_chunk(i):
+        for t in range(3):
+            for m in (2, 1, 0):
+                copy = pltpu.make_async_remote_copy(
+                    src_ref=sources[t].at[:, columns(peers[m], i)],
+                    dst_ref=qkv.at[t, i, my_rows, :],
+                    send_sem=qkv_send.at[t, m, i],
+                    recv_sem=qkv_recv.at[t, m, i],
+                    device_id={"head": peers[m]},
+                    device_id_type=MESH,
+                )
+                copy.start()
+                qkv_copies[t, m, i] = copy
+            copy = pltpu.make_async_copy(
+                sources[t].at[:, columns(me, i)], qkv.at[t, i, my_rows, :], own_sem.at[t, i]
+            )
+            copy.start()
+            own_copies[t, i] = copy
+
+    ahead = min(2, chunks)
+    for i in range(ahead):
+        send_chunk(i)
+
+    dino_copies = []
+    for step in range(1, seq_count):
+        copy = pltpu.make_async_remote_copy(
+            src_ref=dino_ref,
+            dst_ref=dino_all.at[seq],
+            send_sem=dino_send.at[step - 1],
+            recv_sem=dino_recv.at[step - 1],
+            device_id={"seq": lax.rem(seq + step, seq_count)},
+            device_id_type=MESH,
+        )
+        copy.start()
+        dino_copies.append(copy)
+    loads = []
+    for n, (src, dst) in enumerate(
+        (
+            (dino_ref, dino_all.at[seq]),
+            (w_ref, w_v),
+            (res_ref, res_v),
+            (p1_ref, p1_v),
+            (p2_ref, p2_v),
+        )
+    ):
+        copy = pltpu.make_async_copy(src, dst, load_sem.at[n])
+        copy.start()
+        loads.append(copy)
+
+    score_scale = HD ** (-0.5)
+    block = min(256, tokens)
+    blocks = tokens // block
+
+    def attend_chunk(i):
+        def body(n, carry):
+            lanes = pl.ds(pl.multiple_of(lax.div(n, blocks) * HD, HD), HD)
+            part = pl.ds(pl.multiple_of(lax.rem(n, blocks) * block, block), block)
+            scores = lax.dot_general(
+                qkv[0, i, part, lanes],
+                qkv[1, i, :, lanes],
+                (((1,), (1,)), ((), ())),
+                preferred_element_type=jnp.float32,
+            )
+            scores = scores * score_scale
+            top = jnp.max(scores, axis=-1, keepdims=True)
+            exponents = jnp.exp(scores - top)
+            total = jnp.sum(exponents, axis=-1, keepdims=True)
+            mixed = jnp.dot(
+                exponents.astype(jnp.bfloat16),
+                qkv[2, i, :, lanes],
+                preferred_element_type=jnp.float32,
+            )
+            att[me * chunks + i, part, lanes] = (mixed / total).astype(jnp.bfloat16)
+            return carry
+
+        lax.fori_loop(0, (width // HD) * blocks, body, 0)
+
+    att_copies = {}
+
+    def send_att(i):
+        for m in (1, 0):
+            copy = pltpu.make_async_remote_copy(
+                src_ref=att.at[me * chunks + i],
+                dst_ref=att.at[me * chunks + i],
+                send_sem=att_send.at[m, i],
+                recv_sem=att_recv.at[m, i],
+                device_id={"head": peers[m]},
+                device_id_type=MESH,
+            )
+            copy.start()
+            att_copies[m, i] = copy
+
+    fwd_copies = {}
+
+    def forward(i):
+        att_copies[1, i].wait_recv()
+        copy = pltpu.make_async_remote_copy(
+            src_ref=att.at[cross * chunks + i],
+            dst_ref=att.at[cross * chunks + i],
+            send_sem=fwd_send.at[i],
+            recv_sem=fwd_recv.at[i],
+            device_id={"head": sib},
+            device_id_type=MESH,
+        )
+        copy.start()
+        fwd_copies[i] = copy
+
+    tile = 256
+
+    def weight_rows(owner, i):
+        return pl.ds(pl.multiple_of(owner * head_cols + i * width, width), width)
+
+    def accumulate(pieces, first):
+        def body(n, carry):
+            cols = pl.ds(pl.multiple_of(n * tile, tile), tile)
+            total = None if first else acc[:, cols]
+            for owner, i in pieces:
+                term = jnp.dot(
+                    att[owner * chunks + i],
+                    w_v[weight_rows(owner, i), cols],
+                    preferred_element_type=jnp.float32,
+                )
+                total = term if total is None else total + term
+            acc[:, cols] = total
+            return carry
+
+        lax.fori_loop(0, wide // tile, body, 0)
+
+    frame_copies = []
+
+    def pick_frames():
+        for copy in dino_copies:
+            copy.wait_recv()
+        loads[0].wait()
+        held = dino_ref.shape[0]
+        for f in range(frame_sel.shape[0]):
+            total = jnp.zeros(frame_sel.shape[1:], jnp.float32)
+            for r in range(seq_count * held):
+                hit = (slot_ref[r] == seq * held + f).astype(jnp.float32)
+                total = total + hit * dino_all[r // held, r % held].astype(jnp.float32)
+            frame_sel[f] = total.astype(jnp.bfloat16)
+        for m, peer in enumerate(peers):
+            copy = pltpu.make_async_remote_copy(
+                src_ref=frame_sel.at[lax.div(peer, 2)],
+                dst_ref=frame_buf.at[me],
+                send_sem=frame_send.at[m],
+                recv_sem=frame_recv.at[m],
+                device_id={"head": peer},
+                device_id_type=MESH,
+            )
+            copy.start()
+            frame_copies.append(copy)
+        frame_buf[me] = frame_sel[chip]
+
+    def make_target():
+        for copy in frame_copies:
+            copy.wait_recv()
+        patches = lax.broadcasted_iota(jnp.int32, (rows, PPF), 1)
+        counts = jnp.zeros((rows, PPF), jnp.float32)
+        for t in range(TAPS):
+            counts = counts + (taps_ref[:, t : t + 1] == patches).astype(jnp.float32)
+        frame = frame_buf[...].reshape(PPF, frame_buf.shape[2])
+        targ_out[...] = jnp.dot(
+            counts.astype(jnp.bfloat16), frame, preferred_element_type=jnp.float32
+        ) * (1.0 / TAPS)
+
+    last = chunks - 1
+    for i in range(chunks):
+        for t in range(3):
+            for m in range(3):
+                qkv_copies[t, m, i].wait_recv()
+            own_copies[t, i].wait()
+        if i + ahead < chunks:
+            send_chunk(i + ahead)
+        attend_chunk(i)
+        send_att(i)
+        if i == 1:
+            loads[1].wait()
+        if i >= 1:
+            forward(i - 1)
+            att_copies[0, i - 1].wait_recv()
+            pieces = [(me, i - 1), (sib, i - 1), (cross, i - 1)]
+            if i >= 2:
+                fwd_copies[i - 2].wait_recv()
+                pieces.append((diag, i - 2))
+            accumulate(pieces, i == 1)
+        if i == 2:
+            pick_frames()
+    att_copies[0, last].wait_recv()
+    fwd_copies[last - 1].wait_recv()
+    accumulate([(me, last), (sib, last), (diag, last - 1)], False)
+    make_target()
+    loads[2].wait()
+    loads[3].wait()
+    forward(last)
+    fwd_copies[last].wait_recv()
+
+    half = 2 * rows
+    hid_copies = []
+
+    def finish_hidden(which, slot):
+        part = pl.ds(pl.multiple_of(which * half, half), half)
+
+        def body(n, carry):
+            cols = pl.ds(pl.multiple_of(n * tile, tile), tile)
+            total = acc[part, cols]
+            for owner in (cross, diag):
+                total = total + jnp.dot(
+                    att[owner * chunks + last, part, :],
+                    w_v[weight_rows(owner, last), cols],
+                    preferred_element_type=jnp.float32,
+                )
+            total = res_v[part, cols].astype(jnp.float32) + total
+            hid_v[slot, :, cols] = total.astype(jnp.bfloat16)
+            return carry
+
+        lax.fori_loop(0, wide // tile, body, 0)
+        copy = pltpu.make_async_copy(hid_v.at[slot], hid_out.at[part, :], hid_sem.at[slot])
+        copy.start()
+        hid_copies.append(copy)
+
+    def partial_pre(slot):
+        def body(n, carry):
+            cols = pl.ds(pl.multiple_of(n * tile, tile), tile)
+            pre_v[slot, :, cols] = jnp.dot(
+                hid_v[slot], p1_v[:, cols], preferred_element_type=jnp.float32
+            )
+            return carry
+
+        lax.fori_loop(0, units // tile, body, 0)
+
+    def send_part(n, peer):
+        copy = pltpu.make_async_remote_copy(
+            src_ref=part_send.at[n],
+            dst_ref=part_recv.at[n],
+            send_sem=part_ssem.at[n],
+            recv_sem=part_rsem.at[n],
+            device_id={"head": peer},
+            device_id_type=MESH,
+        )
+        copy.start()
+        return copy
+
+    mine = pl.ds(pl.multiple_of(core * rows, rows), rows)
+    theirs = pl.ds(pl.multiple_of((1 - core) * rows, rows), rows)
+    finish_hidden(1 - chip, 0)
+    partial_pre(0)
+    part_send[0] = pre_v[0, theirs, :].astype(jnp.bfloat16)
+    first_part = send_part(0, sib)
+    finish_hidden(chip, 1)
+    first_part.wait_recv()
+    part_send[1] = (pre_v[0, mine, :] + part_recv[0].astype(jnp.float32)).astype(jnp.bfloat16)
+    second_part = send_part(1, cross)
+    partial_pre(1)
+    part_send[2] = pre_v[1, theirs, :].astype(jnp.bfloat16)
+    third_part = send_part(2, sib)
+    loads[4].wait()
+    third_part.wait_recv()
+    second_part.wait_recv()
+    pre_act = (
+        pre_v[1, mine, :] + part_recv[2].astype(jnp.float32) + part_recv[1].astype(jnp.float32)
+    )
+    lift_v[...] = (pre_act / (1.0 + jnp.exp(-pre_act))).astype(jnp.bfloat16)
+
+    def project(n, sums):
+        cols = pl.ds(pl.multiple_of(n * tile, tile), tile)
+        value = jnp.dot(lift_v[...], p2_v[:, cols], preferred_element_type=jnp.float32).astype(
+            jnp.bfloat16
+        )
+        proj_out[:, cols] = value
+        value = value.astype(jnp.float32)
+        target = targ_out[:, cols]
+        inner, proj_sq, target_sq = sums
+        return (
+            inner + jnp.sum(value * target, axis=-1, keepdims=True),
+            proj_sq + jnp.sum(value * value, axis=-1, keepdims=True),
+            target_sq + jnp.sum(target * target, axis=-1, keepdims=True),
+        )
+
+    zero = jnp.zeros((rows, 1), jnp.float32)
+    inner, proj_sq, target_sq = lax.fori_loop(
+        0, p2_v.shape[1] // tile, project, (zero, zero, zero)
+    )
+    cos_out[...] = inner / jnp.sqrt((proj_sq + 1e-06) * (target_sq + 1e-06))
+
+    for copy in hid_copies:
+        copy.wait()
+    for copy in qkv_copies.values():
+        copy.wait_send()
+    for copy in att_copies.values():
+        copy.wait_send()
+    for copy in fwd_copies.values():
+        copy.wait_send()
+    for copy in dino_copies + frame_copies + [first_part, second_part, third_part]:
+        copy.wait_send()
+
+
+def fused_device(
+    query_rows,
+    key_rows,
+    value_rows,
+    residual,
+    out_weight,
+    proj_first,
+    proj_second,
+    dino_feats,
+    slot_frame,
+    patch_taps,
+):
+    seq_count = lax.axis_size("seq")
+    rows, all_cols = query_rows.shape
+    tokens, wide = residual.shape
+    units = proj_first.shape[1]
+    feats = proj_second.shape[1]
+    width = CHUNK_HEADS * HD
+    chunks = all_cols // 4 // width
+    held, part_patches = dino_feats.shape[:2]
+    bf16 = jnp.bfloat16
+    f32 = jnp.float32
+    dma = pltpu.SemaphoreType.DMA
+    any_spec = pl.BlockSpec(memory_space=pl.ANY)
+    vmem_spec = pl.BlockSpec(memory_space=pltpu.VMEM)
+    hidden, projected, target, cosine = pl.pallas_call(
+        functools.partial(fused_kernel, seq_count),
+        out_shape=(
+            jax.ShapeDtypeStruct((tokens, wide), bf16),
+            jax.ShapeDtypeStruct((rows, feats), bf16),
+            jax.ShapeDtypeStruct((rows, feats), f32),
+            jax.ShapeDtypeStruct((rows, 1), f32),
+        ),
+        in_specs=[any_spec] * 8 + [pl.BlockSpec(memory_space=pltpu.SMEM), vmem_spec],
+        out_specs=(any_spec, vmem_spec, vmem_spec, vmem_spec),
+        scratch_shapes=[
+            pltpu.VMEM((3, chunks, tokens, width), bf16),
+            pltpu.VMEM((4 * chunks, tokens, width), bf16),
+            pltpu.VMEM((tokens, wide), f32),
+            pltpu.VMEM(out_weight.shape, bf16),
+            pltpu.VMEM(proj_first.shape, bf16),
+            pltpu.VMEM(proj_second.shape, bf16),
+            pltpu.VMEM((tokens, wide), bf16),
+            pltpu.VMEM((2, 2 * rows, wide), bf16),
+            pltpu.VMEM((2, 2 * rows, units), f32),
+            pltpu.VMEM((rows, units), bf16),
+            pltpu.VMEM((3, rows, units), bf16),
+            pltpu.VMEM((3, rows, units), bf16),
+            pltpu.VMEM((seq_count, held, part_patches, feats), bf16),
+            pltpu.VMEM((held, part_patches, feats), bf16),
+            pltpu.VMEM((4, part_patches, feats), bf16),
+            dma((5,)),
+            dma((3, chunks)),
+            dma((3, 3, chunks)),
+            dma((3, 3, chunks)),
+            dma((2, chunks)),
+            dma((2, chunks)),
+            dma((chunks,)),
+            dma((chunks,)),
+            dma((3,)),
+            dma((3,)),
+            dma((seq_count - 1,)),
+            dma((seq_count - 1,)),
+            dma((3,)),
+            dma((3,)),
+            dma((2,)),
+        ],
+        compiler_params=pltpu.CompilerParams(
+            collective_id=0, has_side_effects=True, vmem_limit_bytes=56 * 1024 * 1024
+        ),
+        cost_estimate=pl.CostEstimate(
+            flops=2 * tokens * (all_cols * wide + wide * units),
+            bytes_accessed=24 * 1024 * 1024,
+            transcendentals=0,
+        ),
+        name="sublayer",
+    )(
+        query_rows,
+        key_rows,
+        value_rows,
+        residual,
+        out_weight,
+        proj_first,
+        proj_second,
+        dino_feats,
+        slot_frame,
+        patch_taps,
+    )
+    return (hidden, projected, target, cosine.reshape(rows))
+
+
 def solution(mesh):
+    body = fused_device if mesh.shape["head"] == 4 else per_device
     return jax.shard_map(
-        per_device,
+        body,
         mesh=mesh,
         in_specs=(
             P(("seq", "head"), None),

time: 188 us -> 92.3 us (0.49)
  Pallas kernels: 0 us -> 84.3 us
  waiting for transfers between devices: 68.4 us -> 0 us
  blocking collectives: 38.4 us -> 0 us
  matrix products: 30 us -> 0 us
  local copies, waits for them, and re-layouts: 23 us -> 5.51 us
  between operations: 14.2 us -> 0.66 us
  starting transfers between devices: 12.9 us -> 0 us
    pallas_call x0 -> x1, Pallas kernels: none -> 84.3 us  [fused_device(): pl.pallas_call(functools.partial(fused_kernel, seq_count), out_shape=(jax...]
    all_gather x2 -> x0, blocking collectives: 38.4 us -> none  [the longest x1 32.3 us: per_device(): everything = lax.all_gather(dino_feats, 'seq', axis=0, tiled=True)]
    all_gather x1 -> x0, waiting for transfers between devices: 35.7 us -> none  [per_device(): lax.all_gather(attended, 'head', axis=1, tiled=True)]
    all_to_all x3 -> x0, waiting for transfers between devices: 32.6 us -> none  [the longest x1 12.3 us: per_device(): lax.all_to_all(key_heads, 'head', split_axis=1, concat_axis=0, tiled=True)]
    dot_general x6 -> x0, matrix products: 22.5 us -> none  [the longest x1 10.8 us: per_device(): jnp.dot(lax.all_gather(attended, 'head', axis=1, tiled=True), out_weight,...]
    all_to_all x3 -> x0, starting transfers between devices: 12.8 us -> none  [the longest x1 4.29 us: per_device(): lax.all_to_all(value_heads, 'head', split_axis=1, concat_axis=0, tiled=True)]
    all_to_all x3 -> x0, local copies, waits for them, and re-layouts: 7.72 us -> none  [the longest x1 3.01 us: per_device(): lax.all_to_all(value_heads, 'head', split_axis=1, concat_axis=0, tiled=True)]
    sub x1 -> x0, matrix products: 7.44 us -> none  [one_window(): exponents = jnp.exp(scores - row_max)]
  transfers between devices with their start and end apart: 5 -> 0, of which waited for: 4 -> 0; matrix products, arithmetic and copies ran while one was open for 7% -> 0% of each run, Pallas kernels for 0% -> 0%
where the time goes in v1:
time: 92.3 us; the launch traced here: 92 us
  Pallas kernels  84.3 us (91%)
  local copies, waits for them, and re-layouts  5.51 us (6%)
  other arithmetic  1.56 us (2%)
    pallas_call x1, Pallas kernels, fused_device(): pl.pallas_call(functools.partial(fused_kernel, seq_count), out_shape=(jax...  84.3 us
    unnamed x8, local copies, waits for them, and re-layouts  5.51 us

profile of v1, /device:TPU:0, one launch (start us, length us, event | category | flops | bytes accessed | tf_op | source)
XLA Modules:
  0.0 92.0 jit_solution(6687394812653867026)
XLA Ops:
  0.6 1.4 %copy.15.taps_ref = s32[128,4]{1,0:T(8,128)} copy(s32[128,4]{0,1:T(4,128)} %param.19) | data formatting | bytes 4096 | tf_op args[9]
  2.0 84.3 %sublayer.1 = (bf16[512,1280]{1,0:T(8,128)(2,1)}, bf16[128,1536]{1,0:T(8,128)(2,1)}, f32[128,1536]{1,0:T(8,128)}, f32[128,1]{1,0:T(8,128)}) custom-call(bf16[128,4096]{1,0:T(8,128)(2,1)} %q_ref.1, bf16[128,4096]{1,0:T(8,128)(2,1)} %k_ref.1, bf16[128,4096]{1,0:T(8,128)(2,1)} %v_ref.1, bf16[512,1280]{1,0:T(8,128)(2,1)} %res_ref.1, bf16[4096,1280]{1,0:T(8,128)(2,1)} %w_ref.1, ...), custom_call_target="tpu_custom_call" | custom-call | flops 6710886400 | bytes 25165824 | tf_op jit(solution)/shard_map/sublayer/pallas_call | solution.py:519
  86.4 0.0 copy-start.1
  86.4 0.0 copy-start
  86.4 1.6 %reduce = f32[128]{0:T(128)} reduce(f32[128,1]{1,0:T(8,128)} %get-tuple-element.11, f32[]{:T(128)} %constant.1), dimensions={1}, to_apply=%get-tuple-element.11.reduce_sub_computation | reduce | bytes 1028 | tf_op jit(solution)/shard_map/sublayer/pallas_call | solution.py:519
  87.9 2.5 %copy.19 = bf16[512,1280]{1,0:T(8,128)(2,1)} copy(bf16[512,1280]{1,0:T(8,128)(2,1)} %get-tuple-element.16) | data formatting | bytes 2621440
  90.4 0.0 copy-done.1
  90.4 0.7 copy.20
  91.1 0.0 copy-done
  91.1 0.9 copy.21
Async XLA Ops:
  86.4 4.0 %copy-start.1 = (bf16[128,1536]{1,0:T(8,128)(2,1)S(1)}, bf16[128,1536]{1,0:T(8,128)(2,1)}, u32[]{:S(2)}) copy-start(bf16[128,1536]{1,0:T(8,128)(2,1)} %get-tuple-element.17) | copy-start | bytes 1179652
  86.4 4.8 %copy-start = (f32[128,1536]{1,0:T(8,128)S(1)}, f32[128,1536]{1,0:T(8,128)}, u32[]{:S(2)}) copy-start(f32[128,1536]{1,0:T(8,128)} %get-tuple-element.18) | copy-start | bytes 2359300

commit v2 on v1

v2 whole, which is shorter than its diff:
```python
import functools

import jax
import jax.numpy as jnp
from jax import lax
from jax.experimental import pallas as pl
from jax.experimental.pallas import tpu as pltpu
from jax.sharding import PartitionSpec as P

HD = 128
PPF = 64
TAPS = 4
BLOCK = 512


def attend(operands):
    query_part, key_part, value_part = operands
    length = query_part.shape[0]
    item_count = query_part.shape[2]
    window_count = length // BLOCK
    score_scale = HD ** (-0.5)
    shaped = (
        query_part[:, 0].reshape(window_count, BLOCK, item_count, HD),
        key_part[:, 0].reshape(window_count, BLOCK, item_count, HD),
        value_part[:, 0].reshape(window_count, BLOCK, item_count, HD),
    )

    def one_window(parts):
        query_block, key_block, value_block = parts
        scores = (
            jnp.einsum("qhd,khd->hqk", query_block, key_block, preferred_element_type=jnp.float32)
            * score_scale
        )
        row_max = jnp.max(scores, axis=-1, keepdims=True)
        exponents = jnp.exp(scores - row_max)
        weights = (exponents / jnp.sum(exponents, axis=-1, keepdims=True)).astype(jnp.bfloat16)
        return jnp.einsum(
            "hqk,khd->qhd", weights, value_block, preferred_element_type=jnp.float32
        ).astype(jnp.bfloat16)

    return lax.map(one_window, shaped).reshape(length, 1, item_count, HD)


def per_device(
    query_rows,
    key_rows,
    value_rows,
    residual,
    out_weight,
    proj_first,
    proj_second,
    dino_feats,
    slot_frame,
    patch_taps,
):
    own_rows = query_rows.shape[0]
    group_count = lax.axis_size("head")
    per_group = query_rows.shape[1] // (HD * group_count)
    query_heads = query_rows.reshape(own_rows, group_count, per_group, HD)
    key_heads = key_rows.reshape(own_rows, group_count, per_group, HD)
    value_heads = value_rows.reshape(own_rows, group_count, per_group, HD)
    attended = attend(
        (
            lax.all_to_all(query_heads, "head", split_axis=1, concat_axis=0, tiled=True),
            lax.all_to_all(key_heads, "head", split_axis=1, concat_axis=0, tiled=True),
            lax.all_to_all(value_heads, "head", split_axis=1, concat_axis=0, tiled=True),
        )
    )
    seq_len = attended.shape[0]
    attended = attended.reshape(seq_len, per_group * HD)
    mixed_sum = jnp.dot(
        lax.all_gather(attended, "head", axis=1, tiled=True),
        out_weight,
        preferred_element_type=jnp.float32,
    )
    hidden = (residual.astype(jnp.float32) + mixed_sum).astype(jnp.bfloat16)
    pre_act = lax.psum_scatter(
        jnp.dot(hidden, proj_first, preferred_element_type=jnp.float32),
        "head",
        scatter_dimension=0,
        tiled=True,
    )
    lifted = jax.nn.silu(pre_act).astype(jnp.bfloat16)
    projected = jnp.dot(lifted, proj_second, preferred_element_type=jnp.float32).astype(
        jnp.bfloat16
    )
    seq_index = lax.axis_index("seq")
    head_index = lax.axis_index("head")
    frames_here = dino_feats.shape[0]
    wanted = seq_index * frames_here + jnp.arange(frames_here, dtype=jnp.int32)
    everything = lax.all_gather(dino_feats, "seq", axis=0, tiled=True)
    picker = (slot_frame[None, :] == wanted[:, None]).astype(jnp.bfloat16)
    frame_part = jnp.einsum(
        "ir,rpz->ipz", picker, everything, preferred_element_type=jnp.float32
    ).astype(jnp.bfloat16)
    whole_frames = lax.all_gather(frame_part, "head", axis=1, tiled=True)
    frame_feat = lax.dynamic_index_in_dim(whole_frames, head_index // 2, 0, keepdims=False)
    patch_ids = jnp.arange(PPF, dtype=jnp.int32)
    tap_counts = jnp.sum(
        (patch_taps[:, :, None] == patch_ids[None, None, :]).astype(jnp.float32), axis=1
    )
    target = jnp.dot(
        tap_counts.astype(jnp.bfloat16), frame_feat, preferred_element_type=jnp.float32
    ) * (1.0 / TAPS)
    proj_float = projected.astype(jnp.float32)
    inner = jnp.sum(proj_float * target, axis=-1)
    proj_sq = jnp.sum(proj_float * proj_float, axis=-1) + 1e-06
    target_sq = jnp.sum(target * target, axis=-1) + 1e-06
    cosine = inner / jnp.sqrt(proj_sq * target_sq)
    return (hidden, projected, target, cosine)


CHUNK_HEADS = 2
ROW_GROUPS = 4
MESH = pl.DeviceIdType.MESH


def fused_kernel(
    seq_count,
    q_ref,
    k_ref,
    v_ref,
    res_ref,
    w_ref,
    p1_ref,
    p2_ref,
    dino_ref,
    slot_ref,
    taps_ref,
    hid_out,
    proj_out,
    targ_out,
    cos_out,
    q_buf,
    kv_buf,
    att,
    acc,
    w_v,
    p1_v,
    p2_v,
    res_v,
    hid_v,
    pre_v,
    lift_v,
    sib_part,
    cross_send,
    cross_part,
    dino_all,
    frame_sel,
    frame_buf,
    load_sem,
    res_sem,
    own_sem,
    qkv_send,
    qkv_recv,
    sib_send,
    sib_recv,
    cross_ssem,
    cross_rsem,
    fwd_send,
    fwd_recv,
    part_send,
    part_recv,
    hop_send,
    hop_recv,
    dino_send,
    dino_recv,
    frame_send,
    frame_recv,
    hid_sem,
):
    seq = lax.axis_index("seq")
    me = lax.axis_index("head")
    chip = lax.div(me, 2)
    core = lax.rem(me, 2)
    sib = 2 * chip + (1 - core)
    cross = 2 * (1 - chip) + core
    diag = 2 * (1 - chip) + (1 - core)
    peers = (sib, cross, diag)
    groups, sub, all_cols = q_ref.shape
    rows = groups * sub
    tokens = 4 * rows
    group_rows = 4 * sub
    head_cols = all_cols // 4
    chunks = q_buf.shape[0]
    width = q_buf.shape[4]
    heads = width // HD
    wide = w_v.shape[1]
    units = p1_v.shape[1]
    tile = 256

    barrier = pltpu.get_barrier_semaphore()
    for peer in peers:
        pl.semaphore_signal(barrier, inc=1, device_id={"head": peer}, device_id_type=MESH)
    for step in range(1, seq_count):
        other = lax.rem(seq + step, seq_count)
        pl.semaphore_signal(barrier, inc=1, device_id={"seq": other}, device_id_type=MESH)
    pl.semaphore_wait(barrier, 3 + seq_count - 1)

    def send(src, dst, ssem, rsem, peer):
        copy = pltpu.make_async_remote_copy(
            src_ref=src,
            dst_ref=dst,
            send_sem=ssem,
            recv_sem=rsem,
            device_id={"head": peer},
            device_id_type=MESH,
        )
        copy.start()
        return copy

    my_rows = pl.ds(pl.multiple_of(me * rows, rows), rows)

    def columns(owner, i):
        return pl.ds(pl.multiple_of(owner * head_cols + i * width, width), width)

    def source(t, owner, i):
        if t == 0:
            return q_ref.at[:, :, columns(owner, i)]
        return (k_ref, v_ref)[t - 1].at[:, columns(owner, i)]

    def landing(t, i):
        if t == 0:
            return q_buf.at[i, :, me]
        return kv_buf.at[t - 1, i, my_rows, :]

    qkv_copies = {}
    own_copies = {}

    def send_chunk(i):
        for t in range(3):
            for m in (2, 1, 0):
                qkv_copies[t, m, i] = send(
                    source(t, peers[m], i),
                    landing(t, i),
                    qkv_send.at[t, m, i],
                    qkv_recv.at[t, m, i],
                    peers[m],
                )
            copy = pltpu.make_async_copy(source(t, me, i), landing(t, i), own_sem.at[t, i])
            copy.start()
            own_copies[t, i] = copy

    ahead = min(2, chunks)
    for i in range(ahead):
        send_chunk(i)

    dino_copies = []
    for step in range(1, seq_count):
        copy = pltpu.make_async_remote_copy(
            src_ref=dino_ref,
            dst_ref=dino_all.at[seq],
            send_sem=dino_send.at[step - 1],
            recv_sem=dino_recv.at[step - 1],
            device_id={"seq": lax.rem(seq + step, seq_count)},
            device_id_type=MESH,
        )
        copy.start()
        dino_copies.append(copy)
    loads = []
    for n, (src, dst) in enumerate(
        ((dino_ref, dino_all.at[seq]), (w_ref, w_v), (p1_ref, p1_v), (p2_ref, p2_v))
    ):
        copy = pltpu.make_async_copy(src, dst, load_sem.at[n])
        copy.start()
        loads.append(copy)
    res_loads = []
    for g in range(groups):
        copy = pltpu.make_async_copy(res_ref.at[:, g], res_v.at[g], res_sem.at[g])
        copy.start()
        res_loads.append(copy)

    score_scale = HD ** (-0.5)

    def attend(i, n, first, count):
        lanes = pl.ds(pl.multiple_of(n * HD, HD), HD)
        query = q_buf[i, pl.ds(first, count), :, :, lanes].reshape(count * group_rows, HD)
        scores = lax.dot_general(
            query,
            kv_buf[0, i, :, lanes],
            (((1,), (1,)), ((), ())),
            preferred_element_type=jnp.float32,
        )
        scores = scores * score_scale
        top = jnp.max(scores, axis=-1, keepdims=True)
        exponents = jnp.exp(scores - top)
        total = jnp.sum(exponents, axis=-1, keepdims=True)
        mixed = jnp.dot(
            exponents.astype(jnp.bfloat16),
            kv_buf[1, i, :, lanes],
            preferred_element_type=jnp.float32,
        )
        mixed = (mixed / total).astype(jnp.bfloat16)
        place = pl.ds(pl.multiple_of(me * head_cols + i * width + n * HD, HD), HD)
        att[pl.ds(first, count), :, place] = mixed.reshape(count, group_rows, HD)

    both = min(2, groups)

    def attend_chunk(i):
        def body(n, carry):
            attend(i, lax.div(n, groups // both), lax.rem(n, groups // both) * both, both)
            return carry

        lax.fori_loop(0, heads * (groups // both), body, 0)

    last = chunks - 1
    early = last * width

    def owned(g, owner, start, size):
        return att.at[g, :, pl.ds(pl.multiple_of(owner * head_cols + start, width), size)]

    att_copies = {}

    def send_att(g, part):
        mine = owned(g, me, 0, early) if part == 0 else owned(g, me, early, width)
        att_copies[1, g, part] = send(
            mine, mine, cross_ssem.at[g, part], cross_rsem.at[g, part], cross
        )
        att_copies[0, g, part] = send(mine, mine, sib_send.at[g, part], sib_recv.at[g, part], sib)

    frame_copies = []

    def pick_frames():
        for copy in dino_copies:
            copy.wait_recv()
        loads[0].wait()
        held = dino_ref.shape[0]
        for f in range(frame_sel.shape[0]):
            total = jnp.zeros(frame_sel.shape[1:], jnp.float32)
            for r in range(seq_count * held):
                hit = (slot_ref[r] == seq * held + f).astype(jnp.float32)
                total = total + hit * dino_all[r // held, r % held].astype(jnp.float32)
            frame_sel[f] = total.astype(jnp.bfloat16)
        for m, (peer, which) in enumerate(((sib, chip), (cross, 1 - chip))):
            frame_copies.append(
                send(
                    frame_sel.at[which],
                    frame_buf.at[me],
                    frame_send.at[m],
                    frame_recv.at[m],
                    peer,
                )
            )
        frame_buf[me] = frame_sel[chip]

    def forward_frames():
        frame_copies[1].wait_recv()
        frame_copies.append(
            send(
                frame_buf.at[cross], frame_buf.at[cross], frame_send.at[2], frame_recv.at[2], sib
            )
        )

    def make_target():
        frame_copies[0].wait_recv()
        frame_copies[2].wait_recv()
        patches = lax.broadcasted_iota(jnp.int32, (PPF, rows), 0)
        counts = jnp.zeros((PPF, rows), jnp.float32)
        for t in range(TAPS):
            counts = counts + (taps_ref[t : t + 1, :] == patches).astype(jnp.float32)
        counts = counts.T.astype(jnp.bfloat16)
        frame = frame_buf[...].reshape(PPF, frame_buf.shape[2])
        targ_out[...] = jnp.dot(counts, frame, preferred_element_type=jnp.float32) * (1.0 / TAPS)

    for i in range(last):
        for t in range(3):
            for m in range(3):
                qkv_copies[t, m, i].wait_recv()
            own_copies[t, i].wait()
        if i + ahead < chunks:
            send_chunk(i + ahead)
        attend_chunk(i)
    send_att(0, 0)
    pick_frames()
    for t in range(3):
        for m in range(3):
            qkv_copies[t, m, last].wait_recv()
        own_copies[t, last].wait()
    for g in range(groups):

        def last_heads(n, carry, g=g):
            attend(last, n, g, 1)
            return carry

        lax.fori_loop(0, heads, last_heads, 0)
        send_att(g, 1)
        if g + 1 < groups:
            send_att(g + 1, 0)
    forward_frames()
    loads[1].wait()

    def products(g, owners, cols):
        total = None
        for owner in owners:
            part = pl.ds(pl.multiple_of(owner * head_cols, head_cols), head_cols)
            term = jnp.dot(
                att[g, :, part], w_v[part, cols], preferred_element_type=jnp.float32
            )
            total = term if total is None else total + term
        return total

    def over_tiles(count, step):
        def body(n, carry):
            step(pl.ds(pl.multiple_of(n * tile, tile), tile))
            return carry

        lax.fori_loop(0, count // tile, body, 0)

    hid_copies = []
    part_copies = {}
    hop_copies = {}
    fwd_copies = {}

    def reduce_hop(g):
        part_copies[g, 0].wait_recv()
        cross_send[g] = (pre_v[g, cross] + sib_part[g, 0]).astype(jnp.bfloat16)
        hop_copies[g] = send(
            cross_send.at[g], cross_part.at[g], hop_send.at[g], hop_recv.at[g], cross
        )

    for g in range(groups):
        for part in range(2):
            att_copies[0, g, part].wait_recv()

        def near(cols, g=g):
            acc[:, cols] = products(g, (me, sib), cols)

        over_tiles(wide, near)
        if g >= 1:
            reduce_hop(g - 1)
        if g == groups - 1:
            make_target()
        for part in range(2):
            att_copies[1, g, part].wait_recv()
        theirs = owned(g, cross, 0, head_cols)
        fwd_copies[g] = send(theirs, theirs, fwd_send.at[g], fwd_recv.at[g], sib)

        def far(cols, g=g):
            acc[:, cols] = acc[:, cols] + products(g, (cross,), cols)

        over_tiles(wide, far)
        fwd_copies[g].wait_recv()
        res_loads[g].wait()

        def close(cols, g=g):
            total = acc[:, cols] + products(g, (diag,), cols)
            total = total.reshape(4, sub, tile) + res_v[g, :, :, cols].astype(jnp.float32)
            hid_v[g, :, :, cols] = total.astype(jnp.bfloat16)

        over_tiles(wide, close)
        copy = pltpu.make_async_copy(hid_v.at[g], hid_out.at[:, g], hid_sem.at[g])
        copy.start()
        hid_copies.append(copy)
        if g == 0:
            loads[2].wait()

        def first_layer(cols, g=g):
            value = jnp.dot(
                hid_v[g].reshape(group_rows, wide), p1_v[:, cols],
                preferred_element_type=jnp.float32,
            )
            pre_v[g, :, :, cols] = value.reshape(4, sub, tile)

        over_tiles(units, first_layer)
        for n, owner in enumerate((diag, sib)):
            part_copies[g, n] = send(
                pre_v.at[g, owner],
                sib_part.at[g, n],
                part_send.at[g, n],
                part_recv.at[g, n],
                sib,
            )
    reduce_hop(groups - 1)
    loads[3].wait()
    for g in range(groups):
        part_copies[g, 1].wait_recv()
        hop_copies[g].wait_recv()
        pre_act = pre_v[g, me] + sib_part[g, 1] + cross_part[g].astype(jnp.float32)
        lift_v[pl.ds(g * sub, sub), :] = (pre_act / (1.0 + jnp.exp(-pre_act))).astype(
            jnp.bfloat16
        )

    def project(n, sums):
        cols = pl.ds(pl.multiple_of(n * tile, tile), tile)
        value = jnp.dot(lift_v[...], p2_v[:, cols], preferred_element_type=jnp.float32).astype(
            jnp.bfloat16
        )
        proj_out[:, cols] = value
        value = value.astype(jnp.float32)
        target = targ_out[:, cols]
        inner, proj_sq, target_sq = sums
        return (
            inner + jnp.sum(value * target, axis=-1, keepdims=True),
            proj_sq + jnp.sum(value * value, axis=-1, keepdims=True),
            target_sq + jnp.sum(target * target, axis=-1, keepdims=True),
        )

    zero = jnp.zeros((rows, 1), jnp.float32)
    inner, proj_sq, target_sq = lax.fori_loop(
        0, p2_v.shape[1] // tile, project, (zero, zero, zero)
    )
    cosine = inner / jnp.sqrt((proj_sq + 1e-06) * (target_sq + 1e-06))
    cos_out[...] = jnp.broadcast_to(cosine, (rows, rows)).T[0:1, :]

    for copy in hid_copies:
        copy.wait()
    for copies in (qkv_copies, att_copies, fwd_copies, part_copies, hop_copies):
        for copy in copies.values():
            copy.wait_send()
    for copy in dino_copies + frame_copies:
        copy.wait_send()


def fused_device(
    query_rows,
    key_rows,
    value_rows,
    residual,
    out_weight,
    proj_first,
    proj_second,
    dino_feats,
    slot_frame,
    patch_taps,
):
    seq_count = lax.axis_size("seq")
    rows, all_cols = query_rows.shape
    tokens, wide = residual.shape
    units = proj_first.shape[1]
    feats = proj_second.shape[1]
    width = CHUNK_HEADS * HD
    chunks = all_cols // 4 // width
    groups = ROW_GROUPS
    sub = rows // groups
    held, part_patches = dino_feats.shape[:2]
    bf16 = jnp.bfloat16
    f32 = jnp.float32
    dma = pltpu.SemaphoreType.DMA
    any_spec = pl.BlockSpec(memory_space=pl.ANY)
    vmem_spec = pl.BlockSpec(memory_space=pltpu.VMEM)
    hidden, projected, target, cosine = pl.pallas_call(
        functools.partial(fused_kernel, seq_count),
        out_shape=(
            jax.ShapeDtypeStruct((4, groups, sub, wide), bf16),
            jax.ShapeDtypeStruct((rows, feats), bf16),
            jax.ShapeDtypeStruct((rows, feats), f32),
            jax.ShapeDtypeStruct((1, rows), f32),
        ),
        in_specs=[any_spec] * 8 + [pl.BlockSpec(memory_space=pltpu.SMEM), vmem_spec],
        out_specs=(any_spec, vmem_spec, vmem_spec, vmem_spec),
        scratch_shapes=[
            pltpu.VMEM((chunks, groups, 4, sub, width), bf16),
            pltpu.VMEM((2, chunks, tokens, width), bf16),
            pltpu.VMEM((groups, 4 * sub, all_cols), bf16),
            pltpu.VMEM((4 * sub, wide), f32),
            pltpu.VMEM(out_weight.shape, bf16),
            pltpu.VMEM(proj_first.shape, bf16),
            pltpu.VMEM(proj_second.shape, bf16),
            pltpu.VMEM((groups, 4, sub, wide), bf16),
            pltpu.VMEM((groups, 4, sub, wide), bf16),
            pltpu.VMEM((groups, 4, sub, units), f32),
            pltpu.VMEM((rows, units), bf16),
            pltpu.VMEM((groups, 2, sub, units), f32),
            pltpu.VMEM((groups, sub, units), bf16),
            pltpu.VMEM((groups, sub, units), bf16),
            pltpu.VMEM((seq_count, held, part_patches, feats), bf16),
            pltpu.VMEM((held, part_patches, feats), bf16),
            pltpu.VMEM((4, part_patches, feats), bf16),
            dma((4,)),
            dma((groups,)),
            dma((3, chunks)),
            dma((3, 3, chunks)),
            dma((3, 3, chunks)),
            dma((groups, 2)),
            dma((groups, 2)),
            dma((groups, 2)),
            dma((groups, 2)),
            dma((groups,)),
            dma((groups,)),
            dma((groups, 2)),
            dma((groups, 2)),
            dma((groups,)),
            dma((groups,)),
            dma((seq_count - 1,)),
            dma((seq_count - 1,)),
            dma((3,)),
            dma((3,)),
            dma((groups,)),
        ],
        compiler_params=pltpu.CompilerParams(
            collective_id=0, has_side_effects=True, vmem_limit_bytes=56 * 1024 * 1024
        ),
        cost_estimate=pl.CostEstimate(
            flops=2 * tokens * (all_cols * wide + wide * units),
            bytes_accessed=24 * 1024 * 1024,
            transcendentals=0,
        ),
        name="sublayer",
    )(
        query_rows.reshape(groups, sub, all_cols),
        key_rows,
        value_rows,
        residual.reshape(4, groups, sub, wide),
        out_weight,
        proj_first,
        proj_second,
        dino_feats,
        slot_frame,
        patch_taps.T,
    )
    return (hidden.reshape(tokens, wide), projected, target, cosine.reshape(rows))


def solution(mesh):
    body = fused_device if mesh.shape["head"] == 4 else per_device
    return jax.shard_map(
        body,
        mesh=mesh,
        in_specs=(
            P(("seq", "head"), None),
            P(("seq", "head"), None),
            P(("seq", "head"), None),
            P("seq", "head"),
            P(None, "head"),
            P("head", None),
            P(),
            P("seq", "head", None),
            P(),
            P(("seq", "head"), None),
        ),
        out_specs=(
            P("seq", "head"),
            P(("seq", "head"), None),
            P(("seq", "head"), None),
            P(("seq", "head")),
        ),
        check_vma=False,
    )
```

time: 92.3 us -> 85.3 us (0.924)
  Pallas kernels: 84.3 us -> 79.7 us
  other arithmetic: 1.56 us -> 0 us
    pallas_call x1, Pallas kernels: 84.3 us -> 79.7 us  [fused_device(): pl.pallas_call(functools.partial(fused_kernel, seq_count), out_shape=(jax...]
    pallas_call x1 -> x0, other arithmetic: 1.56 us -> none  [fused_device(): pl.pallas_call(functools.partial(fused_kernel, seq_count), out_shape=(jax...]
    unnamed x8 -> x10, local copies, waits for them, and re-layouts: 5.51 us -> 4.7 us
where the time goes in v2:
time: 85.3 us; the launch traced here: 85.1 us
  Pallas kernels  79.7 us (93%)
  local copies, waits for them, and re-layouts  4.7 us (6%)
    pallas_call x1, Pallas kernels, fused_device(): pl.pallas_call(functools.partial(fused_kernel, seq_count), out_shape=(jax...  79.7 us
    unnamed x10, local copies, waits for them, and re-layouts  4.7 us

profile of v2, /device:TPU:0, one launch (start us, length us, event | category | flops | bytes accessed | tf_op | source)
XLA Modules:
  0.0 85.1 jit_solution(7909359237877656589)
XLA Ops:
  0.6 79.7 %sublayer.1 = (bf16[4,4,32,1280]{3,2,1,0:T(8,128)(2,1)}, bf16[128,1536]{1,0:T(8,128)(2,1)}, f32[128,1536]{1,0:T(8,128)}, f32[1,128]{1,0:T(1,128)}) custom-call(bf16[4,32,4096]{2,1,0:T(8,128)(2,1)} %bitcast.7, bf16[128,4096]{1,0:T(8,128)(2,1)} %k_ref.1, bf16[128,4096]{1,0:T(8,128)(2,1)} %v_ref.1, bf16[4,4,32,1280]{3,2,1,0:T(8,128)(2,1)} %bitcast.6, ...), custom_call_target="tpu_custom_call" | custom-call | flops 6710886400 | bytes 25165824 | tf_op jit(solution)/shard_map/sublayer/pallas_call | solution.py:541
  80.4 0.0 copy-start.1
  80.4 0.0 copy-start
  80.4 0.0 copy-start.2
  80.4 2.5 %copy.18 = bf16[512,1280]{1,0:T(8,128)(2,1)} copy(bf16[512,1280]{1,0:T(8,128)(2,1)} %bitcast.5) | data formatting | bytes 2621440
  83.0 0.0 copy-done.1
  83.0 0.7 copy.19
  83.7 0.0 copy-done
  83.7 0.9 %copy.20 = f32[128,1536]{1,0:T(8,128)} copy(f32[128,1536]{1,0:T(8,128)S(1)} %copy-done) | data formatting | bytes 1572864
  84.6 0.0 copy-done.2
  84.6 0.5 copy.21
Async XLA Ops:
  80.4 2.6 %copy-start.1 = (bf16[128,1536]{1,0:T(8,128)(2,1)S(1)}, bf16[128,1536]{1,0:T(8,128)(2,1)}, u32[]{:S(2)}) copy-start(bf16[128,1536]{1,0:T(8,128)(2,1)} %get-tuple-element.17) | copy-start | bytes 1179652
  80.4 3.3 %copy-start = (f32[128,1536]{1,0:T(8,128)S(1)}, f32[128,1536]{1,0:T(8,128)}, u32[]{:S(2)}) copy-start(f32[128,1536]{1,0:T(8,128)} %get-tuple-element.18) | copy-start | bytes 2359300
  80.4 4.2 %copy-start.2 = (f32[1,128]{1,0:T(1,128)S(1)}, f32[1,128]{1,0:T(1,128)}, u32[]{:S(2)}) copy-start(f32[1,128]{1,0:T(1,128)} %get-tuple-element.11) | copy-start | bytes 1540

commit v3 on v2

--- a/solution.py
+++ b/solution.py
@@ -123,25 +123,20 @@
     res_ref,
     w_ref,
     p1_ref,
-    p2_ref,
     dino_ref,
     slot_ref,
-    taps_ref,
     hid_out,
-    proj_out,
-    targ_out,
-    cos_out,
+    lift_out,
+    frame_out,
     q_buf,
     kv_buf,
     att,
     acc,
     w_v,
     p1_v,
-    p2_v,
     res_v,
     hid_v,
     pre_v,
-    lift_v,
     sib_part,
     cross_send,
     cross_part,
@@ -259,7 +254,7 @@
         dino_copies.append(copy)
     loads = []
     for n, (src, dst) in enumerate(
-        ((dino_ref, dino_all.at[seq]), (w_ref, w_v), (p1_ref, p1_v), (p2_ref, p2_v))
+        ((dino_ref, dino_all.at[seq]), (w_ref, w_v), (p1_ref, p1_v))
     ):
         copy = pltpu.make_async_copy(src, dst, load_sem.at[n])
         copy.start()
@@ -312,7 +307,12 @@
     att_copies = {}
 
     def send_att(g, part):
-        mine = owned(g, me, 0, early) if part == 0 else owned(g, me, early, width)
+        if part == 0:
+            mine = owned(g, me, 0, early)
+        elif g == 0:
+            mine = owned(g, me, early, width)
+        else:
+            mine = owned(g, me, 0, head_cols)
         att_copies[1, g, part] = send(
             mine, mine, cross_ssem.at[g, part], cross_rsem.at[g, part], cross
         )
@@ -351,16 +351,10 @@
             )
         )
 
-    def make_target():
+    def place_frames():
         frame_copies[0].wait_recv()
         frame_copies[2].wait_recv()
-        patches = lax.broadcasted_iota(jnp.int32, (PPF, rows), 0)
-        counts = jnp.zeros((PPF, rows), jnp.float32)
-        for t in range(TAPS):
-            counts = counts + (taps_ref[t : t + 1, :] == patches).astype(jnp.float32)
-        counts = counts.T.astype(jnp.bfloat16)
-        frame = frame_buf[...].reshape(PPF, frame_buf.shape[2])
-        targ_out[...] = jnp.dot(counts, frame, preferred_element_type=jnp.float32) * (1.0 / TAPS)
+        frame_out[...] = frame_buf[...].reshape(frame_out.shape)
 
     for i in range(last):
         for t in range(3):
@@ -371,7 +365,6 @@
             send_chunk(i + ahead)
         attend_chunk(i)
     send_att(0, 0)
-    pick_frames()
     for t in range(3):
         for m in range(3):
             qkv_copies[t, m, last].wait_recv()
@@ -384,9 +377,7 @@
 
         lax.fori_loop(0, heads, last_heads, 0)
         send_att(g, 1)
-        if g + 1 < groups:
-            send_att(g + 1, 0)
-    forward_frames()
+    pick_frames()
     loads[1].wait()
 
     def products(g, owners, cols):
@@ -419,7 +410,7 @@
         )
 
     for g in range(groups):
-        for part in range(2):
+        for part in (0, 1) if g == 0 else (1,):
             att_copies[0, g, part].wait_recv()
 
         def near(cols, g=g):
@@ -428,9 +419,7 @@
         over_tiles(wide, near)
         if g >= 1:
             reduce_hop(g - 1)
-        if g == groups - 1:
-            make_target()
-        for part in range(2):
+        for part in (0, 1) if g == 0 else (1,):
             att_copies[1, g, part].wait_recv()
         theirs = owned(g, cross, 0, head_cols)
         fwd_copies[g] = send(theirs, theirs, fwd_send.at[g], fwd_recv.at[g], sib)
@@ -470,37 +459,16 @@
                 part_recv.at[g, n],
                 sib,
             )
+    forward_frames()
     reduce_hop(groups - 1)
-    loads[3].wait()
+    place_frames()
     for g in range(groups):
         part_copies[g, 1].wait_recv()
         hop_copies[g].wait_recv()
         pre_act = pre_v[g, me] + sib_part[g, 1] + cross_part[g].astype(jnp.float32)
-        lift_v[pl.ds(g * sub, sub), :] = (pre_act / (1.0 + jnp.exp(-pre_act))).astype(
+        lift_out[pl.ds(g * sub, sub), :] = (pre_act / (1.0 + jnp.exp(-pre_act))).astype(
             jnp.bfloat16
         )
-
-    def project(n, sums):
-        cols = pl.ds(pl.multiple_of(n * tile, tile), tile)
-        value = jnp.dot(lift_v[...], p2_v[:, cols], preferred_element_type=jnp.float32).astype(
-            jnp.bfloat16
-        )
-        proj_out[:, cols] = value
-        value = value.astype(jnp.float32)
-        target = targ_out[:, cols]
-        inner, proj_sq, target_sq = sums
-        return (
-            inner + jnp.sum(value * target, axis=-1, keepdims=True),
-            proj_sq + jnp.sum(value * value, axis=-1, keepdims=True),
-            target_sq + jnp.sum(target * target, axis=-1, keepdims=True),
-        )
-
-    zero = jnp.zeros((rows, 1), jnp.float32)
-    inner, proj_sq, target_sq = lax.fori_loop(
-        0, p2_v.shape[1] // tile, project, (zero, zero, zero)
-    )
-    cosine = inner / jnp.sqrt((proj_sq + 1e-06) * (target_sq + 1e-06))
-    cos_out[...] = jnp.broadcast_to(cosine, (rows, rows)).T[0:1, :]
 
     for copy in hid_copies:
         copy.wait()
@@ -509,6 +477,80 @@
             copy.wait_send()
     for copy in dino_copies + frame_copies:
         copy.wait_send()
+
+
+def project_kernel(
+    hid_ref,
+    lift_ref,
+    frame_ref,
+    taps_ref,
+    p2_ref,
+    hid_out,
+    proj_out,
+    targ_out,
+    cos_out,
+    hid_v,
+    p2_v,
+    proj_v,
+    targ_v,
+    hid_in_sem,
+    hid_out_sem,
+    p2_sem,
+    out_sem,
+):
+    rows = lift_ref.shape[0]
+    tile = 256
+    tiles = p2_v.shape[1] // tile
+    parts = hid_v.shape[0]
+    p2_loads = []
+    for n in range(tiles):
+        cols = pl.ds(n * tile, tile)
+        copy = pltpu.make_async_copy(p2_ref.at[:, cols], p2_v.at[:, cols], p2_sem.at[n])
+        copy.start()
+        p2_loads.append(copy)
+    hid_loads = []
+    for n in range(parts):
+        copy = pltpu.make_async_copy(hid_ref.at[n], hid_v.at[n], hid_in_sem.at[n])
+        copy.start()
+        hid_loads.append(copy)
+    patches = lax.broadcasted_iota(jnp.int32, (PPF, rows), 0)
+    counts = jnp.zeros((PPF, rows), jnp.float32)
+    for t in range(TAPS):
+        counts = counts + (taps_ref[t : t + 1, :] == patches).astype(jnp.float32)
+    counts = counts.T.astype(jnp.bfloat16)
+    targ_v[...] = jnp.dot(counts, frame_ref[...], preferred_element_type=jnp.float32) * (
+        1.0 / TAPS
+    )
+    stores = [pltpu.make_async_copy(targ_v, targ_out, out_sem.at[0])]
+    stores[0].start()
+    inner = jnp.zeros((rows, 1), jnp.float32)
+    proj_sq = jnp.zeros((rows, 1), jnp.float32)
+    target_sq = jnp.zeros((rows, 1), jnp.float32)
+    for n in range(tiles):
+        cols = pl.ds(n * tile, tile)
+        p2_loads[n].wait()
+        value = jnp.dot(
+            lift_ref[...], p2_v[:, cols], preferred_element_type=jnp.float32
+        ).astype(jnp.bfloat16)
+        proj_v[:, cols] = value
+        value = value.astype(jnp.float32)
+        target = targ_v[:, cols]
+        inner = inner + jnp.sum(value * target, axis=-1, keepdims=True)
+        proj_sq = proj_sq + jnp.sum(value * value, axis=-1, keepdims=True)
+        target_sq = target_sq + jnp.sum(target * target, axis=-1, keepdims=True)
+        if n == 0:
+            for m in range(parts):
+                hid_loads[m].wait()
+                copy = pltpu.make_async_copy(hid_v.at[m], hid_out.at[m], hid_out_sem.at[m])
+                copy.start()
+                stores.append(copy)
+    copy = pltpu.make_async_copy(proj_v, proj_out, out_sem.at[1])
+    copy.start()
+    stores.append(copy)
+    cosine = inner / jnp.sqrt((proj_sq + 1e-06) * (target_sq + 1e-06))
+    cos_out[...] = jnp.broadcast_to(cosine, (rows, rows)).T[0:1, :]
+    for copy in stores:
+        copy.wait()
 
 
 def fused_device(
@@ -538,16 +580,15 @@
     dma = pltpu.SemaphoreType.DMA
     any_spec = pl.BlockSpec(memory_space=pl.ANY)
     vmem_spec = pl.BlockSpec(memory_space=pltpu.VMEM)
-    hidden, projected, target, cosine = pl.pallas_call(
+    hidden, lifted, frames = pl.pallas_call(
         functools.partial(fused_kernel, seq_count),
         out_shape=(
             jax.ShapeDtypeStruct((4, groups, sub, wide), bf16),
-            jax.ShapeDtypeStruct((rows, feats), bf16),
-            jax.ShapeDtypeStruct((rows, feats), f32),
-            jax.ShapeDtypeStruct((1, rows), f32),
+            jax.ShapeDtypeStruct((rows, units), bf16),
+            jax.ShapeDtypeStruct((4 * part_patches, feats), bf16),
         ),
-        in_specs=[any_spec] * 8 + [pl.BlockSpec(memory_space=pltpu.SMEM), vmem_spec],
-        out_specs=(any_spec, vmem_spec, vmem_spec, vmem_spec),
+        in_specs=[any_spec] * 7 + [pl.BlockSpec(memory_space=pltpu.SMEM)],
+        out_specs=(any_spec, vmem_spec, vmem_spec),
         scratch_shapes=[
             pltpu.VMEM((chunks, groups, 4, sub, width), bf16),
             pltpu.VMEM((2, chunks, tokens, width), bf16),
@@ -555,18 +596,16 @@
             pltpu.VMEM((4 * sub, wide), f32),
             pltpu.VMEM(out_weight.shape, bf16),
             pltpu.VMEM(proj_first.shape, bf16),
-            pltpu.VMEM(proj_second.shape, bf16),
             pltpu.VMEM((groups, 4, sub, wide), bf16),
             pltpu.VMEM((groups, 4, sub, wide), bf16),
             pltpu.VMEM((groups, 4, sub, units), f32),
-            pltpu.VMEM((rows, units), bf16),
             pltpu.VMEM((groups, 2, sub, units), f32),
             pltpu.VMEM((groups, sub, units), bf16),
             pltpu.VMEM((groups, sub, units), bf16),
             pltpu.VMEM((seq_count, held, part_patches, feats), bf16),
             pltpu.VMEM((held, part_patches, feats), bf16),
             pltpu.VMEM((4, part_patches, feats), bf16),
-            dma((4,)),
+            dma((3,)),
             dma((groups,)),
             dma((3, chunks)),
             dma((3, 3, chunks)),
@@ -603,11 +642,35 @@
         residual.reshape(4, groups, sub, wide),
         out_weight,
         proj_first,
-        proj_second,
         dino_feats,
         slot_frame,
-        patch_taps.T,
-    )
+    )
+    hidden, projected, target, cosine = pl.pallas_call(
+        project_kernel,
+        out_shape=(
+            jax.ShapeDtypeStruct(hidden.shape, bf16),
+            jax.ShapeDtypeStruct((rows, feats), bf16),
+            jax.ShapeDtypeStruct((rows, feats), f32),
+            jax.ShapeDtypeStruct((1, rows), f32),
+        ),
+        in_specs=[any_spec, vmem_spec, vmem_spec, vmem_spec, any_spec],
+        out_specs=(any_spec, any_spec, any_spec, vmem_spec),
+        scratch_shapes=[
+            pltpu.VMEM(hidden.shape, bf16),
+            pltpu.VMEM(proj_second.shape, bf16),
+            pltpu.VMEM((rows, feats), bf16),
+            pltpu.VMEM((rows, feats), f32),
+            dma((4,)),
+            dma((4,)),
+            dma((feats // 256,)),
+            dma((2,)),
+        ],
+        compiler_params=pltpu.CompilerParams(vmem_limit_bytes=56 * 1024 * 1024),
+        cost_estimate=pl.CostEstimate(
+            flops=2 * rows * units * feats, bytes_accessed=8 * 1024 * 1024, transcendentals=0
+        ),
+        name="project",
+    )(hidden, lifted, frames, patch_taps.T, proj_second)
     return (hidden.reshape(tokens, wide), projected, target, cosine.reshape(rows))
 
 

time: 85.3 us -> 83.9 us (0.984)
  local copies, waits for them, and re-layouts: 4.7 us -> 0 us
  Pallas kernels: 79.7 us -> 83.1 us
    pallas_call x0 -> x1, Pallas kernels: none -> 6.78 us  [fused_device(): pl.pallas_call(project_kernel, out_shape=(jax.ShapeDtypeStruct(hidden.sha...]
    unnamed x10 -> x0, local copies, waits for them, and re-layouts: 4.7 us -> none
    pallas_call x1, Pallas kernels: 79.7 us -> 76.3 us  [fused_device(): pl.pallas_call(functools.partial(fused_kernel, seq_count), out_shape=(jax...]
where the time goes in v3:
time: 83.9 us; the launch traced here: 83.8 us
  Pallas kernels  83.1 us (99%)
    pallas_call x1, Pallas kernels, fused_device(): pl.pallas_call(functools.partial(fused_kernel, seq_count), out_shape=(jax...  76.3 us
    pallas_call x1, Pallas kernels, fused_device(): pl.pallas_call(project_kernel, out_shape=(jax.ShapeDtypeStruct(hidden.sha...  6.78 us

profile of v3, /device:TPU:0, one launch (start us, length us, event | category | flops | bytes accessed | tf_op | source)
XLA Modules:
  0.0 83.8 jit_solution(5796442142409040013)
XLA Ops:
  0.6 76.3 %sublayer.1 = (bf16[4,4,32,1280]{3,2,1,0:T(8,128)(2,1)}, bf16[128,1024]{1,0:T(8,128)(2,1)}, bf16[64,1536]{1,0:T(8,128)(2,1)}) custom-call(bf16[4,32,4096]{2,1,0:T(8,128)(2,1)} %bitcast.8, bf16[128,4096]{1,0:T(8,128)(2,1)} %k_ref.1, bf16[128,4096]{1,0:T(8,128)(2,1)} %v_ref.1, bf16[4,4,32,1280]{3,2,1,0:T(8,128)(2,1)} %bitcast.6, bf16[4096,1280]{1,0:T(8,128)(2,1)} %w_ref.1, ...), custom_call_target="tpu_custom_call" | custom-call | flops 6710886400 | bytes 25165824 | tf_op jit(solution)/shard_map/sublayer/pallas_call | solution.py:583
  77.0 6.8 %project.1 = (bf16[4,4,32,1280]{3,2,1,0:T(8,128)(2,1)}, bf16[128,1536]{1,0:T(8,128)(2,1)}, f32[128,1536]{1,0:T(8,128)}, f32[1,128]{1,0:T(1,128)}) custom-call(bf16[4,4,32,1280]{3,2,1,0:T(8,128)(2,1)} %get-tuple-element.11.hid_ref, bf16[128,1024]{1,0:T(8,128)(2,1)} %get-tuple-element.12.lift_ref, bf16[64,1536]{1,0:T(8,128)(2,1)} %get-tuple-element.13.frame_ref, ...), custom_call_target="tpu_custom_call" | custom-call | flops 402653184 | bytes 8388608 | tf_op jit(solution)/shard_map/project/pallas_call | solution.py:648

commit v4 on v2

--- a/solution.py
+++ b/solution.py
@@ -312,7 +312,12 @@
     att_copies = {}
 
     def send_att(g, part):
-        mine = owned(g, me, 0, early) if part == 0 else owned(g, me, early, width)
+        if part == 0:
+            mine = owned(g, me, 0, early)
+        elif g == 0:
+            mine = owned(g, me, early, width)
+        else:
+            mine = owned(g, me, 0, head_cols)
         att_copies[1, g, part] = send(
             mine, mine, cross_ssem.at[g, part], cross_rsem.at[g, part], cross
         )
@@ -371,7 +376,6 @@
             send_chunk(i + ahead)
         attend_chunk(i)
     send_att(0, 0)
-    pick_frames()
     for t in range(3):
         for m in range(3):
             qkv_copies[t, m, last].wait_recv()
@@ -384,9 +388,7 @@
 
         lax.fori_loop(0, heads, last_heads, 0)
         send_att(g, 1)
-        if g + 1 < groups:
-            send_att(g + 1, 0)
-    forward_frames()
+    pick_frames()
     loads[1].wait()
 
     def products(g, owners, cols):
@@ -419,7 +421,7 @@
         )
 
     for g in range(groups):
-        for part in range(2):
+        for part in (0, 1) if g == 0 else (1,):
             att_copies[0, g, part].wait_recv()
 
         def near(cols, g=g):
@@ -428,9 +430,7 @@
         over_tiles(wide, near)
         if g >= 1:
             reduce_hop(g - 1)
-        if g == groups - 1:
-            make_target()
-        for part in range(2):
+        for part in (0, 1) if g == 0 else (1,):
             att_copies[1, g, part].wait_recv()
         theirs = owned(g, cross, 0, head_cols)
         fwd_copies[g] = send(theirs, theirs, fwd_send.at[g], fwd_recv.at[g], sib)
@@ -470,8 +470,10 @@
                 part_recv.at[g, n],
                 sib,
             )
+    forward_frames()
     reduce_hop(groups - 1)
     loads[3].wait()
+    make_target()
     for g in range(groups):
         part_copies[g, 1].wait_recv()
         hop_copies[g].wait_recv()
@@ -509,6 +511,25 @@
             copy.wait_send()
     for copy in dino_copies + frame_copies:
         copy.wait_send()
+
+
+def place_kernel(hid, proj, targ, cos, hid_out, proj_out, targ_out, cos_out, hid_v, proj_v, targ_v, load_sem, store_sem):
+    moves = [(hid.at[n], hid_v.at[n], hid_out.at[n]) for n in range(hid.shape[0])]
+    moves += [(proj, proj_v, proj_out), (targ, targ_v, targ_out)]
+    loads = [
+        pltpu.make_async_copy(src, held, load_sem.at[n]) for n, (src, held, _) in enumerate(moves)
+    ]
+    stores = [
+        pltpu.make_async_copy(held, dst, store_sem.at[n]) for n, (_, held, dst) in enumerate(moves)
+    ]
+    for load in loads:
+        load.start()
+    cos_out[...] = cos[...]
+    for load, store in zip(loads, stores):
+        load.wait()
+        store.start()
+    for store in stores:
+        store.wait()
 
 
 def fused_device(
@@ -608,6 +629,22 @@
         slot_frame,
         patch_taps.T,
     )
+    parts = (hidden, projected, target, cosine)
+    hidden, projected, target, cosine = pl.pallas_call(
+        place_kernel,
+        out_shape=tuple(jax.ShapeDtypeStruct(part.shape, part.dtype) for part in parts),
+        in_specs=[any_spec] * 3 + [vmem_spec],
+        out_specs=(any_spec,) * 3 + (vmem_spec,),
+        scratch_shapes=[
+            pltpu.VMEM(hidden.shape, bf16),
+            pltpu.VMEM((rows, feats), bf16),
+            pltpu.VMEM((rows, feats), f32),
+            dma((6,)),
+            dma((6,)),
+        ],
+        compiler_params=pltpu.CompilerParams(vmem_limit_bytes=56 * 1024 * 1024),
+        name="place",
+    )(*parts)
     return (hidden.reshape(tokens, wide), projected, target, cosine.reshape(rows))
 
 

time: 85.3 us -> 83.3 us (0.977)
  local copies, waits for them, and re-layouts: 4.7 us -> 0 us
  Pallas kernels: 79.7 us -> 82.5 us
    unnamed x10 -> x0, local copies, waits for them, and re-layouts: 4.7 us -> none
    pallas_call x0 -> x1, Pallas kernels: none -> 3.77 us  [fused_device(): pl.pallas_call(place_kernel, out_shape=tuple((jax.ShapeDtypeStruct(part.s...]
    pallas_call x1, Pallas kernels: 79.7 us -> 78.7 us  [fused_device(): pl.pallas_call(functools.partial(fused_kernel, seq_count), out_shape=(jax...]
where the time goes in v4:
time: 83.3 us; the launch traced here: 83.1 us
  Pallas kernels  82.5 us (99%)
    pallas_call x1, Pallas kernels, fused_device(): pl.pallas_call(functools.partial(fused_kernel, seq_count), out_shape=(jax...  78.7 us
    pallas_call x1, Pallas kernels, fused_device(): pl.pallas_call(place_kernel, out_shape=tuple((jax.ShapeDtypeStruct(part.s...  3.77 us

profile of v4, /device:TPU:0, one launch (start us, length us, event | category | flops | bytes accessed | tf_op | source)
XLA Modules:
  0.0 83.1 jit_solution(8959725729012528032)
XLA Ops:
  0.6 78.7 %sublayer.1 = (bf16[4,4,32,1280]{3,2,1,0:T(8,128)(2,1)}, bf16[128,1536]{1,0:T(8,128)(2,1)}, f32[128,1536]{1,0:T(8,128)}, f32[1,128]{1,0:T(1,128)}) custom-call(bf16[4,32,4096]{2,1,0:T(8,128)(2,1)} %bitcast.7, bf16[128,4096]{1,0:T(8,128)(2,1)} %k_ref.1, bf16[128,4096]{1,0:T(8,128)(2,1)} %v_ref.1, bf16[4,4,32,1280]{3,2,1,0:T(8,128)(2,1)} %bitcast.5, ...), custom_call_target="tpu_custom_call" | custom-call | flops 6710886400 | bytes 25165824 | tf_op jit(solution)/shard_map/sublayer/pallas_call | solution.py:562
  79.3 3.8 %place.1 = (bf16[4,4,32,1280]{3,2,1,0:T(8,128)(2,1)}, bf16[128,1536]{1,0:T(8,128)(2,1)}, f32[128,1536]{1,0:T(8,128)}, f32[1,128]{1,0:T(1,128)}) custom-call(bf16[4,4,32,1280]{3,2,1,0:T(8,128)(2,1)} %get-tuple-element.12.hid, bf16[128,1536]{1,0:T(8,128)(2,1)} %get-tuple-element.13.proj, f32[128,1536]{1,0:T(8,128)} %get-tuple-element.14.targ, ...), custom_call_target="tpu_custom_call" | custom-call | tf_op jit(solution)/shard_map/place/pallas_call | solution.py:633

commit v5 on v4

--- a/solution.py
+++ b/solution.py
@@ -514,7 +514,11 @@
 
 
 def place_kernel(hid, proj, targ, cos, hid_out, proj_out, targ_out, cos_out, hid_v, proj_v, targ_v, load_sem, store_sem):
-    moves = [(hid.at[n], hid_v.at[n], hid_out.at[n]) for n in range(hid.shape[0])]
+    moves = [
+        (hid.at[n, g], hid_v.at[n, g], hid_out.at[n, g])
+        for n in range(hid.shape[0])
+        for g in range(hid.shape[1])
+    ]
     moves += [(proj, proj_v, proj_out), (targ, targ_v, targ_out)]
     loads = [
         pltpu.make_async_copy(src, held, load_sem.at[n]) for n, (src, held, _) in enumerate(moves)
@@ -639,8 +643,8 @@
             pltpu.VMEM(hidden.shape, bf16),
             pltpu.VMEM((rows, feats), bf16),
             pltpu.VMEM((rows, feats), f32),
-            dma((6,)),
-            dma((6,)),
+            dma((4 * groups + 2,)),
+            dma((4 * groups + 2,)),
         ],
         compiler_params=pltpu.CompilerParams(vmem_limit_bytes=56 * 1024 * 1024),
         name="place",

time: 83.3 us -> 83.6 us (level)
  no operation moved by 1% of the time
where the time goes in v5:
time: 83.6 us; the launch traced here: 83.4 us
  Pallas kernels  82.8 us (99%)
    pallas_call x1, Pallas kernels, fused_device(): pl.pallas_call(functools.partial(fused_kernel, seq_count), out_shape=(jax...  78.7 us
    pallas_call x1, Pallas kernels, fused_device(): pl.pallas_call(place_kernel, out_shape=tuple((jax.ShapeDtypeStruct(part.s...  4.09 us

profile of v5, /device:TPU:0, one launch (start us, length us, event | category | flops | bytes accessed | tf_op | source)
XLA Modules:
  0.0 83.4 jit_solution(3023450922543089177)
XLA Ops:
  0.6 78.7 %sublayer.1 = (bf16[4,4,32,1280]{3,2,1,0:T(8,128)(2,1)}, bf16[128,1536]{1,0:T(8,128)(2,1)}, f32[128,1536]{1,0:T(8,128)}, f32[1,128]{1,0:T(1,128)}) custom-call(bf16[4,32,4096]{2,1,0:T(8,128)(2,1)} %bitcast.7, bf16[128,4096]{1,0:T(8,128)(2,1)} %k_ref.1, bf16[128,4096]{1,0:T(8,128)(2,1)} %v_ref.1, bf16[4,4,32,1280]{3,2,1,0:T(8,128)(2,1)} %bitcast.5, ...), custom_call_target="tpu_custom_call" | custom-call | flops 6710886400 | bytes 25165824 | tf_op jit(solution)/shard_map/sublayer/pallas_call | solution.py:566
  79.3 4.1 %place.1 = (bf16[4,4,32,1280]{3,2,1,0:T(8,128)(2,1)}, bf16[128,1536]{1,0:T(8,128)(2,1)}, f32[128,1536]{1,0:T(8,128)}, f32[1,128]{1,0:T(1,128)}) custom-call(bf16[4,4,32,1280]{3,2,1,0:T(8,128)(2,1)} %get-tuple-element.12.hid, bf16[128,1536]{1,0:T(8,128)(2,1)} %get-tuple-element.13.proj, f32[128,1536]{1,0:T(8,128)} %get-tuple-element.14.targ, ...), custom_call_target="tpu_custom_call" | custom-call | tf_op jit(solution)/shard_map/place/pallas_call | solution.py:637
